TPU v7x, 32 devices: a whole 2x2x4 slice. The times are simulated.
32 devices in a mesh: groups: 2 (over y), node: 4 (over x, core), local: 4 (over z).
Axes of the slice: x: 2, y: 2, z: 4, core: 2. Of those that a mesh axis runs over, the one named last changes fastest.
Arguments:
- tokens: bfloat16 [256, 3584], P(('groups', 'node', 'local')), parts along dimension 0, may hold values from -6 to 6
- expert_ids: int32 [256, 4], P(('groups', 'node', 'local')), parts along dimension 0, may hold values from 0 to 3, all different within a row; in each aligned block of 8 rows (0 to 7, 8 to 15, ...) at most 8 rows name the same one
- gate_values: float32 [256, 4], P(('groups', 'node', 'local')), parts along dimension 0, may hold values from 0.05 to 1
- shared_gate: bfloat16 [3584, 1024], P(None, 'local'), may hold values from -0.09375 to 0.09375
- shared_up: bfloat16 [3584, 1024], P(None, 'local'), may hold values from -0.09375 to 0.09375
- shared_down: bfloat16 [1024, 3584], P('local'), may hold values from -0.1875 to 0.1875
- expert_gate: bfloat16 [16, 3584, 256], P(('node', 'local')), may hold values from -0.09375 to 0.09375
- expert_up: bfloat16 [16, 3584, 256], P(('node', 'local')), may hold values from -0.09375 to 0.09375
- expert_down: bfloat16 [16, 256, 3584], P(('node', 'local')), may hold values from -0.1875 to 0.1875
Outputs:
- mixed: bfloat16 [256, 3584], P(('groups', 'node', 'local')), parts along dimension 0
There are 2 independent parts, one for each index of `groups`. A program takes and returns all parts, laid end to end along the dimension named above; an argument that names none is the same for every part. Nothing has to cross between parts.
Inputs may be any that keep to these rules, and one draw needn't show every extreme that they name: `expert_ids`: each row names 4 different experts. Among the 8 rows of one device (aligned blocks), no expert is named by more than 8 rows.
All inputs are finite; a program needn't handle non-finite values.
Results may differ from a plain program's by a relative error of at most 0.0055.
Values may be sent and summed in bfloat16 or wider, within the bound.
A program may use at most 64 MiB of HBM per device.

v0:
```python
import jax
import jax.numpy as jnp
from jax import lax
from jax.sharding import PartitionSpec as P

SHARDS = 4


def run_block(rows, w_gate, w_up, w_down):
    gate_part = jnp.dot(rows, w_gate, preferred_element_type=jnp.float32)
    up_part = jnp.dot(rows, w_up, preferred_element_type=jnp.float32)
    hidden = (jax.nn.silu(gate_part) * up_part).astype(jnp.bfloat16)
    return jnp.dot(hidden, w_down, preferred_element_type=jnp.float32)


def shards(
    tokens,
    expert_ids,
    gate_values,
    shared_gate,
    shared_up,
    shared_down,
    expert_gate,
    expert_up,
    expert_down,
):
    tok_dev, model_width = tokens.shape
    top_count = expert_ids.shape[1]
    node_count = lax.axis_size("node")
    local_count = lax.axis_size("local")
    expert_count = node_count * local_count // SHARDS
    capacity = min(tok_dev, max(2, 3 * tok_dev * top_count // (2 * expert_count)))
    shared_terms = run_block(
        lax.all_gather(tokens, "local", axis=0, tiled=True), shared_gate, shared_up, shared_down
    )
    shared_out = lax.psum_scatter(shared_terms, "local", scatter_dimension=0, tiled=True)
    chosen = expert_ids[:, :, None] == jnp.arange(expert_count, dtype=jnp.int32)
    onehot = jnp.any(chosen, axis=1).astype(jnp.float32)
    weight_table = jnp.sum(jnp.where(chosen, gate_values[:, :, None], jnp.float32(0.0)), axis=1)
    position = jnp.cumsum(onehot, axis=0) - onehot
    slot_iota = jnp.arange(capacity).astype(jnp.float32)
    picker = onehot[:, :, None] * (position[:, :, None] == slot_iota).astype(jnp.float32)
    slot_rows = jnp.einsum(
        "tec,td->ecd", picker.astype(jnp.bfloat16), tokens, preferred_element_type=jnp.float32
    ).astype(jnp.bfloat16)
    outgoing = jnp.repeat(slot_rows, SHARDS, axis=0)
    row_block = lax.all_to_all(outgoing, ("node", "local"), split_axis=0, concat_axis=0, tiled=True)
    leading = row_block.shape[:-1]
    flat_rows = row_block.reshape(-1, model_width)
    result = run_block(flat_rows, expert_gate[0], expert_up[0], expert_down[0])
    partial_out = result.astype(jnp.bfloat16).reshape(leading + (model_width,))
    returned = lax.all_to_all(
        partial_out, ("node", "local"), split_axis=0, concat_axis=0, tiled=True
    )
    expert_result = jnp.sum(
        returned.astype(jnp.float32).reshape(expert_count, SHARDS, capacity, model_width), axis=1
    )
    scaled = picker * weight_table[:, :, None]
    routed = jnp.einsum("tec,ecd->td", scaled, expert_result, precision=lax.Precision.HIGHEST)
    return (shared_out + routed).astype(jnp.bfloat16)


def solution(mesh):
    return jax.shard_map(
        shards,
        mesh=mesh,
        in_specs=(
            P(("groups", "node", "local"), None),
            P(("groups", "node", "local"), None),
            P(("groups", "node", "local"), None),
            P(None, "local"),
            P(None, "local"),
            P("local", None),
            P(("node", "local"), None, None),
            P(("node", "local"), None, None),
            P(("node", "local"), None, None),
        ),
        out_specs=P(("groups", "node", "local"), None),
        check_vma=False,
    )
```

profile of v0, /device:TPU:0, one launch (start us, length us, event | category | flops | bytes accessed | tf_op | source)
XLA Modules:
  0.0 115.7 jit_solution(13965969410831023559)
XLA Ops:
  6.5 0.0 copy-start
  6.5 0.8 fusion.44
  7.4 0.2 reduce_window_sum.11
  7.6 0.0 copy-start.1
  7.6 1.3 %convolution_convert_fusion.1 = bf16[4,8,3584]{2,1,0:T(8,128)(2,1)S(1)} fusion(bf16[8,3584]{1,0:T(8,128)(2,1)} %param.9, f32[8,4]{0,1:T(4,128)S(1)} %convert_element_type.42, f32[8]{0:T(128)S(1)} %iota_convert_fusion, f32[8,4]{0,1:T(4,128)S(1)} %convert_subtract_fusion), kind=kOutput, calls=%fused_computation.2 | convolution fusion | flops 1950208 | bytes 287008 | tf_op jit(solution)/shard_map/tec,td->ecd/dot_general | solution.py:43
  8.9 0.1 broadcast_in_dim.24
  8.9 31.3 %all_to_all.10 = bf16[16,8,3584]{2,1,0:T(8,128)(2,1)S(1)} all-to-all(bf16[16,8,3584]{2,1,0:T(8,128)(2,1)S(1)} %bitcast.43), channel_id=1, replica_groups=mesh['groups'=2,'node'=4,'local'=4] {'node','local'}, dimensions={0} | all-to-all | bytes 1835008 | tf_op jit(solution)/shard_map/all_to_all | solution.py:47
  40.2 0.0 copy-done.1
  40.2 0.4 fusion.6
  40.7 0.0 copy-done
  40.7 3.6 %fusion = bf16[16,8,3584]{2,1,0:T(8,128)(2,1)} fusion(bf16[1,256,3584]{2,1,0:T(8,128)(2,1)S(1)} %copy-done, bf16[1,3584,256]{2,1,0:T(8,128)(2,1)} %param.16, bf16[16,8,3584]{2,1,0:T(8,128)(2,1)S(1)} %all_to_all.10, f32[128,256]{1,0:T(8,128)S(1)} %fusion.6), kind=kOutput, calls=%fused_computation.1 | convolution fusion | flops 470417408 | bytes 5636096 | tf_op jit(solution)/shard_map/dot_general | solution.py:13
  44.3 0.0 copy-start.2
  44.3 3.8 %all-to-all-start.1 = ((bf16[16,8,3584]{2,1,0:T(8,128)(2,1)}), bf16[16,8,3584]{2,1,0:T(8,128)(2,1)S(1)}, u32[]{:S(2)}, u32[]{:S(2)}) async-start(bf16[16,8,3584]{2,1,0:T(8,128)(2,1)} %fusion), calls=%async_computation.2 | async-start | bytes 1835008 | tf_op jit(solution)/shard_map/all_to_all | solution.py:52
  48.1 0.0 reduce-scatter.2.cloned.1.call-start
  48.1 0.0 copy-done.2
  48.1 30.6 %all_gather.3 = bf16[32,3584]{1,0:T(8,128)(2,1)S(1)} all-gather(bf16[8,3584]{1,0:T(8,128)(2,1)S(1)} %copy-done.2), channel_id=1, replica_groups=mesh['groups'=2,'node'=4,'local'=4] {'local'}, dimensions={0}, use_global_device_ids=true | all-gather | bytes 286720 | tf_op jit(solution)/shard_map/all_gather | solution.py:34
  78.7 1.9 %fusion.49 = f32[32,256]{1,0:T(8,128)S(1)} fusion(bf16[32,3584]{1,0:T(8,128)(2,1)S(1)} %all_gather.3, bf16[3584,256]{1,0:T(8,128)(2,1)} %param.12), kind=kOutput, calls=%fused_computation.52 | convolution fusion | flops 58720256 | bytes 2097152 | tf_op jit(solution)/shard_map/dot_general | solution.py:10
  80.6 0.0 copy-start.3
  80.6 0.0 copy-start.4
  80.6 4.0 %fusion.15 = f32[32,3584]{1,0:T(8,128)} fusion(bf16[256,3584]{1,0:T(8,128)(2,1)} %param.14, bf16[32,3584]{1,0:T(8,128)(2,1)S(1)} %all_gather.3, bf16[3584,256]{1,0:T(8,128)(2,1)} %param.13, f32[32,256]{1,0:T(8,128)S(1)} %fusion.49), kind=kOutput, calls=%fused_computation.16 | convolution fusion | flops 117489664 | bytes 4390912 | tf_op jit(solution)/shard_map/dot_general | solution.py:13
  84.6 0.0 reduce-scatter.2.cloned.1.call-update
  84.7 0.0 copy-done.3
  84.7 0.0 copy-done.4
  84.7 0.0 all-to-all-done.1
  84.7 0.1 convert_reduce_fusion
  84.8 21.4 %reduce-scatter.2.cloned.1.call-done = f32[8,3584]{1,0:T(8,128)} async-done(((f32[32,3584]{1,0:T(8,128)}), f32[8,3584]{1,0:T(8,128)}) %reduce-scatter.2.cloned.1.call-update) | async-done | bytes 114704 | tf_op jit(solution)/shard_map/reduce_scatter | solution.py:36
  106.3 2.6 %fusion.2 = bf16[8,3584]{1,0:T(8,128)(2,1)} fusion(f32[8,3584]{1,0:T(8,128)} %reduce-scatter.2.cloned.1.call-done, f32[4,8,3584]{2,1,0:T(8,128)S(1)} %convert_reduce_fusion, f32[8,4]{0,1:T(4,128)S(1)} %select_reduce_fusion, f32[8,4]{0,1:T(4,128)S(1)} %convert_element_type.42, f32[8]{0:T(128)S(1)} %iota_convert_fusion, f32[8,4]{0,1:T(4,128)S(1)} %convert_subtract_fusion), kind=kOutput, calls=%fused_computation.5 | convolution fusion | flops 11068160 | bytes 631200 | tf_op jit(solution)/shard_map/tec,ecd->td/dot_general | solution.py:59
  (4 shorter events, 0.0 us)
Async XLA Ops:
  6.5 34.1 %copy-start = (bf16[1,256,3584]{2,1,0:T(8,128)(2,1)S(1)}, bf16[1,256,3584]{2,1,0:T(8,128)(2,1)}, u32[]{:S(2)}) copy-start(bf16[1,256,3584]{2,1,0:T(8,128)(2,1)} %param.17) | copy-start | bytes 5505028
  7.6 32.7 %copy-start.1 = (bf16[1,3584,256]{2,1,0:T(8,128)(2,1)S(1)}, bf16[1,3584,256]{2,1,0:T(8,128)(2,1)}, u32[]{:S(2)}) copy-start(bf16[1,3584,256]{2,1,0:T(8,128)(2,1)} %param.15) | copy-start | bytes 5505028
  44.3 3.8 %copy-start.2 = (bf16[8,3584]{1,0:T(8,128)(2,1)S(1)}, bf16[8,3584]{1,0:T(8,128)(2,1)}, u32[]{:S(2)}) copy-start(bf16[8,3584]{1,0:T(8,128)(2,1)} %param.9) | copy-start | bytes 172036
  44.3 40.4 %all-to-all-start.1 = ((bf16[16,8,3584]{2,1,0:T(8,128)(2,1)}), bf16[16,8,3584]{2,1,0:T(8,128)(2,1)S(1)}, u32[]{:S(2)}, u32[]{:S(2)}) async-start(bf16[16,8,3584]{2,1,0:T(8,128)(2,1)} %fusion), calls=%async_computation.2 | async-start | bytes 1835008 | tf_op jit(solution)/shard_map/all_to_all | solution.py:52
  48.1 58.2 %reduce-scatter.2.cloned.1.call-start = ((), (), s32[]{:S(2)}) async-start(), calls=%async_computation.3 | async-start | bytes 573440 | tf_op jit(solution)/shard_map/reduce_scatter | solution.py:36
  80.6 4.0 %copy-start.3 = (s32[8,4]{0,1:T(4,128)S(1)}, s32[8,4]{0,1:T(4,128)}, u32[]{:S(2)}) copy-start(s32[8,4]{0,1:T(4,128)} %param.10) | copy-start | bytes 388
  80.6 4.0 %copy-start.4 = (f32[8,4]{0,1:T(4,128)S(1)}, f32[8,4]{0,1:T(4,128)}, u32[]{:S(2)}) copy-start(f32[8,4]{0,1:T(4,128)} %param.11) | copy-start | bytes 388
Sparse Core Ops, SparseCore 0:
  84.8 21.4 reduce-scatter.1
where the time goes:
time: 116 us
  blocking collectives  61.9 us (53%)
  waiting for transfers between devices  21.4 us (18%)
  matrix products  13.8 us (12%)
  between operations  13.5 us (12%)
  starting transfers between devices  3.81 us (3%)
  other arithmetic  1.18 us (1%)
    all_to_all x1, blocking collectives, shards(): lax.all_to_all(outgoing, ('node', 'local'), split_axis=0, concat_axis=0,...  31.3 us
    all_gather x1, blocking collectives, shards(): lax.all_gather(tokens, 'local', axis=0, tiled=True)  30.6 us
    reduce_scatter x1, waiting for transfers between devices, shards(): lax.psum_scatter(shared_terms, 'local', scatter_dimension=0, tiled=True)  21.4 us
    dot_general x2, matrix products, run_block(): return jnp.dot(hidden, w_down, preferred_element_type=jnp.float32)  7.6 us
    all_to_all x1, starting transfers between devices, shards(): lax.all_to_all(partial_out, ('node', 'local'), split_axis=0, concat_axis=...  3.76 us
    dot_general x1, matrix products, shards(): jnp.einsum('tec,ecd->td', scaled, expert_result, precision=lax.Precision....  2.56 us
  transfers between devices with their start and end apart: 2, of which 1 were waited for; matrix products, arithmetic and copies ran while one was open for 5% of the time, Pallas kernels for 0%

commit v1 on v0

--- a/solution.py
+++ b/solution.py
@@ -1,9 +1,14 @@
+import functools
+
 import jax
 import jax.numpy as jnp
 from jax import lax
+from jax.experimental import pallas as pl
+from jax.experimental.pallas import tpu as pltpu
 from jax.sharding import PartitionSpec as P
 
 SHARDS = 4
+MESH = pl.DeviceIdType.MESH
 
 
 def run_block(rows, w_gate, w_up, w_down):
@@ -13,7 +18,7 @@
     return jnp.dot(hidden, w_down, preferred_element_type=jnp.float32)
 
 
-def shards(
+def sparse_shards(
     tokens,
     expert_ids,
     gate_values,
@@ -60,6 +65,239 @@
     return (shared_out + routed).astype(jnp.bfloat16)
 
 
+def flip(value, bits):
+    bit = 1
+    while bit <= bits:
+        if bits & bit:
+            value = value + bit - 2 * bit * ((value // bit) % 2)
+        bit *= 2
+    return value
+
+
+def is_power(n):
+    return n & (n - 1) == 0
+
+
+def dense_kernel(
+    dims,
+    tok_ref, ids_ref, val_ref, sg_ref, su_ref, sd_ref, eg_ref, eu_ref, ed_ref,
+    out_ref,
+    rows, sg, su, sd, eg, eu, ed,
+    keep, sib_out, sib_in, x_out, x_in, z_out, z_in,
+    load_sem, send_sem, recv_sem,
+):
+    nodes, locals_, width, experts = dims
+    tok = tok_ref.shape[0]
+    node, local = lax.axis_index("node"), lax.axis_index("local")
+    evens = range(0, nodes, 2)
+    far = range(2, nodes, 2)
+    order = list(range(locals_ - 1, 0, -1))
+
+    count = iter(range(1 << 16))
+    id_z = {k: next(count) for k in order}
+    id_x = {(r, k): next(count) for r in far for k in range(locals_)}
+    id_s = {(r, k): next(count) for r in evens for k in range(locals_)}
+    id_rs = {(r, k): next(count) for r in evens for k in range(locals_)}
+    id_rx = {(r, k): next(count) for r in far for k in range(locals_)}
+    id_rz = {k: next(count) for k in order}
+
+    loads = []
+    for i, (src, dst) in enumerate((
+        (tok_ref, rows.at[0, 0, :, pl.ds(0, width)]),
+        (eg_ref.at[0], eg), (eu_ref.at[0], eu), (ed_ref.at[0], ed),
+        (sg_ref, sg), (su_ref, su), (sd_ref, sd),
+    )):
+        loads.append(pltpu.make_async_copy(src, dst, load_sem.at[i]))
+        loads[-1].start()
+
+    def at_local(k):
+        return {"local": flip(local, k)}
+
+    def at_node(r):
+        return {"node": flip(node, r)}
+
+    partners = [at_local(k) for k in order] + [at_node(r) for r in far] + [at_node(1)]
+    barrier = pltpu.get_barrier_semaphore()
+    for where in partners:
+        pl.semaphore_signal(barrier, inc=1, device_id=where, device_id_type=MESH)
+
+    lane = lax.broadcasted_iota(jnp.int32, (tok, 128), 1)
+    lane_expert = lax.rem(lane, experts)
+    weight = jnp.zeros((tok, 128), jnp.float32)
+    for k in range(ids_ref.shape[1]):
+        weight = weight + jnp.where(
+            ids_ref[:, k:k + 1] == lane_expert, val_ref[:, k:k + 1], jnp.float32(0.0)
+        )
+    high = weight.astype(jnp.bfloat16).astype(jnp.float32)
+    middle = (weight - high).astype(jnp.bfloat16).astype(jnp.float32)
+    low = weight - high - middle
+    terms = jnp.where(
+        lane < experts, high,
+        jnp.where(lane < 2 * experts, middle, jnp.where(lane < 3 * experts, low, 0.0)),
+    )
+    rows[0, 0, :, width:width + 128] = terms.astype(jnp.bfloat16)
+    loads[0].wait()
+    pl.semaphore_wait(barrier, len(partners))
+
+    started = []
+
+    def send(src, dst, number, where):
+        copy = pltpu.make_async_remote_copy(
+            src_ref=src, dst_ref=dst,
+            send_sem=send_sem.at[number], recv_sem=recv_sem.at[number],
+            device_id=where, device_id_type=MESH,
+        )
+        copy.start()
+        started.append(copy)
+        return copy
+
+    along_z, along_x, to_core = {}, {}, {}
+    for k in order:
+        along_z[k] = send(rows.at[0, 0], rows.at[0, k], id_z[k], at_local(k))
+
+    def pass_on(k):
+        for r in far:
+            along_x[r, k] = send(rows.at[0, k], rows.at[r, k], id_x[r, k], at_node(r))
+        to_core[0, k] = send(rows.at[0, k], rows.at[1, k], id_s[0, k], at_node(1))
+
+    arrival = list(range(locals_))
+    pass_on(0)
+    for k in arrival[1:]:
+        along_z[k].wait_recv()
+        pass_on(k)
+
+    own_expert = (node * locals_ + local) // SHARDS
+
+    def block(x, w_gate, w_up, w_down):
+        g = jnp.dot(x, w_gate[...], preferred_element_type=jnp.float32)
+        u = jnp.dot(x, w_up[...], preferred_element_type=jnp.float32)
+        h = (g / (1.0 + jnp.exp(-g)) * u).astype(jnp.bfloat16)
+        return jnp.dot(h, w_down[...], preferred_element_type=jnp.float32)
+
+    def partial(r):
+        held = rows[r].astype(jnp.float32).reshape(locals_ * tok, width + 128)
+        x = held[:, :width].astype(jnp.bfloat16)
+        tail = held[:, width:]
+        lanes = lax.broadcasted_iota(jnp.int32, tail.shape, 1)
+        mine = (lax.rem(lanes, experts) == own_expert) & (lanes < 3 * experts)
+        factor = jnp.sum(jnp.where(mine, tail, 0.0), axis=1, keepdims=True)
+        y = block(x, eg, eu, ed) * factor
+        if r == 0:
+            y = y + block(x, sg, su, sd)
+        return y.reshape(locals_, tok, width)
+
+    core_sums = {}
+
+    def do_chunk(r):
+        y = partial(r)
+        if r % 2:
+            sib_out[r // 2] = y.astype(jnp.bfloat16)
+            for k in order + [0]:
+                core_sums[r - 1, k] = send(
+                    sib_out.at[r // 2, k], sib_in.at[r // 2, k], id_rs[r - 1, k], at_node(1)
+                )
+        else:
+            keep[r // 2] = y
+
+    for load in loads[1:]:
+        load.wait()
+    do_chunk(0)
+    for r in far:
+        for k in arrival:
+            along_x[r, k].wait_recv()
+            to_core[r, k] = send(rows.at[r, k], rows.at[r + 1, k], id_s[r, k], at_node(1))
+    for k in arrival:
+        to_core[0, k].wait_recv()
+    do_chunk(1)
+    for r in far:
+        do_chunk(r)
+        for k in arrival:
+            to_core[r, k].wait_recv()
+        do_chunk(r + 1)
+
+    x_sums, z_sums = {}, {}
+    for r in far:
+        for k in order + [0]:
+            core_sums[r, k].wait_recv()
+            x_out[r // 2 - 1, k] = (
+                keep[r // 2, k] + sib_in[r // 2, k].astype(jnp.float32)
+            ).astype(jnp.bfloat16)
+            x_sums[r, k] = send(
+                x_out.at[r // 2 - 1, k], x_in.at[r // 2 - 1, k], id_rx[r, k], at_node(r)
+            )
+    for k in order + [0]:
+        core_sums[0, k].wait_recv()
+        total = keep[0, k] + sib_in[0, k].astype(jnp.float32)
+        for r in far:
+            x_sums[r, k].wait_recv()
+            total = total + x_in[r // 2 - 1, k].astype(jnp.float32)
+        if k:
+            z_out[k] = total.astype(jnp.bfloat16)
+            z_sums[k] = send(z_out.at[k], z_in.at[k], id_rz[k], at_local(k))
+    for k in reversed(order):
+        z_sums[k].wait_recv()
+        total = total + z_in[k].astype(jnp.float32)
+    out_ref[...] = total.astype(jnp.bfloat16)
+
+    for copy in started:
+        copy.wait_send()
+
+
+def dense_shards(*args):
+    tokens, expert_ids = args[0], args[1]
+    tok, width = tokens.shape
+    hidden, shared_hidden = args[6].shape[2], args[3].shape[1]
+    nodes, locals_ = lax.axis_size("node"), lax.axis_size("local")
+    experts = nodes * locals_ // SHARDS
+    pairs = nodes // 2
+    copies = (locals_ - 1) * 2 + (pairs - 1) * locals_ * 2 + pairs * locals_ * 2
+    bf16, f32 = jnp.bfloat16, jnp.float32
+    any_spec, vmem_spec = pl.BlockSpec(memory_space=pl.ANY), pl.BlockSpec(memory_space=pltpu.VMEM)
+    return pl.pallas_call(
+        functools.partial(dense_kernel, (nodes, locals_, width, experts)),
+        out_shape=jax.ShapeDtypeStruct((tok, width), bf16),
+        in_specs=[any_spec, vmem_spec, vmem_spec] + [any_spec] * 6,
+        out_specs=vmem_spec,
+        scratch_shapes=[
+            pltpu.VMEM((nodes, locals_, tok, width + 128), bf16),
+            pltpu.VMEM((width, shared_hidden), bf16),
+            pltpu.VMEM((width, shared_hidden), bf16),
+            pltpu.VMEM((shared_hidden, width), bf16),
+            pltpu.VMEM((width, hidden), bf16),
+            pltpu.VMEM((width, hidden), bf16),
+            pltpu.VMEM((hidden, width), bf16),
+            pltpu.VMEM((pairs, locals_, tok, width), f32),
+            pltpu.VMEM((pairs, locals_, tok, width), bf16),
+            pltpu.VMEM((pairs, locals_, tok, width), bf16),
+            pltpu.VMEM((pairs - 1, locals_, tok, width), bf16),
+            pltpu.VMEM((pairs - 1, locals_, tok, width), bf16),
+            pltpu.VMEM((locals_, tok, width), bf16),
+            pltpu.VMEM((locals_, tok, width), bf16),
+            pltpu.SemaphoreType.DMA((7,)),
+            pltpu.SemaphoreType.DMA((copies,)),
+            pltpu.SemaphoreType.DMA((copies,)),
+        ],
+        compiler_params=pltpu.CompilerParams(
+            collective_id=0, has_side_effects=True, vmem_limit_bytes=48 << 20
+        ),
+        cost_estimate=pl.CostEstimate(
+            flops=6 * tok * nodes * locals_ * width * hidden,
+            bytes_accessed=2 * 3 * width * (hidden + shared_hidden),
+            transcendentals=0,
+        ),
+    )(*args)
+
+
+def shards(*args):
+    expert_ids = args[1]
+    nodes, locals_ = lax.axis_size("node"), lax.axis_size("local")
+    experts = nodes * locals_ // SHARDS
+    every_expert = expert_ids.shape[1] == experts and 3 * experts <= 128
+    if every_expert and nodes >= 4 and is_power(nodes) and is_power(locals_):
+        return dense_shards(*args)
+    return sparse_shards(*args)
+
+
 def solution(mesh):
     return jax.shard_map(
         shards,

time: 116 us -> 38 us (0.33)
  blocking collectives: 61.9 us -> 0 us
  Pallas kernels: 0 us -> 30.2 us
  waiting for transfers between devices: 21.4 us -> 0 us
  matrix products: 13.8 us -> 0 us
  between operations: 13.5 us -> 0.01 us
  local copies, waits for them, and re-layouts: 0.09 us -> 7.45 us
  starting transfers between devices: 3.81 us -> 0 us
  other arithmetic: 1.18 us -> 0 us
    all_to_all x1 -> x0, blocking collectives: 31.3 us -> none  [shards(): lax.all_to_all(outgoing, ('node', 'local'), split_axis=0, concat_axis=0,...]
    all_gather x1 -> x0, blocking collectives: 30.6 us -> none  [shards(): lax.all_gather(tokens, 'local', axis=0, tiled=True)]
    pallas_call x0 -> x1, Pallas kernels: none -> 30.2 us  [dense_shards(): pl.pallas_call(functools.partial(dense_kernel, (nodes, locals_, width, ex...]
    reduce_scatter x1 -> x0, waiting for transfers between devices: 21.4 us -> none  [shards(): lax.psum_scatter(shared_terms, 'local', scatter_dimension=0, tiled=True)]
    dot_general x6 -> x0, matrix products: 13.8 us -> none  [the longest x2 7.6 us: run_block(): return jnp.dot(hidden, w_down, preferred_element_type=jnp.float32)]
    unnamed x10 -> x11, local copies, waits for them, and re-layouts: 0.03 us -> 7.45 us
    all_to_all x1 -> x0, starting transfers between devices: 3.76 us -> none  [shards(): lax.all_to_all(partial_out, ('node', 'local'), split_axis=0, concat_axis=...]
  transfers between devices with their start and end apart: 2 -> 0, of which waited for: 1 -> 0; matrix products, arithmetic and copies ran while one was open for 5% -> 0% of each run, Pallas kernels for 0% -> 0%
where the time goes in v1:
time: 38 us; the launch traced here: 37.7 us
  Pallas kernels  30.2 us (79%)
  local copies, waits for them, and re-layouts  7.45 us (20%)
    pallas_call x1, Pallas kernels, dense_shards(): pl.pallas_call(functools.partial(dense_kernel, (nodes, locals_, width, ex...  30.2 us
    unnamed x11, local copies, waits for them, and re-layouts  7.45 us

profile of v1, /device:TPU:0, one launch (start us, length us, event | category | flops | bytes accessed | tf_op | source)
XLA Modules:
  0.0 37.7 jit_solution(8869975758273763312)
XLA Ops:
  0.0 0.8 %copy.10.ids_ref = s32[8,4]{1,0:T(8,128)S(1)} copy(s32[8,4]{0,1:T(4,128)} %param.10) | data formatting | bytes 256 | tf_op args[1]
  0.8 0.8 %copy.11.val_ref = f32[8,4]{1,0:T(8,128)S(1)} copy(f32[8,4]{0,1:T(4,128)} %param.11) | data formatting | bytes 256 | tf_op args[2]
  1.5 0.0 copy-start
  1.5 1.5 %copy-done = bf16[3584,256]{1,0:T(8,128)(2,1)S(1)} copy-done((bf16[3584,256]{1,0:T(8,128)(2,1)S(1)}, bf16[3584,256]{1,0:T(8,128)(2,1)}, u32[]{:S(2)}) %copy-start) | copy-done | bytes 1835032
  3.0 0.0 copy-start.1
  3.0 1.5 %copy-done.1 = bf16[3584,256]{1,0:T(8,128)(2,1)S(1)} copy-done((bf16[3584,256]{1,0:T(8,128)(2,1)S(1)}, bf16[3584,256]{1,0:T(8,128)(2,1)}, u32[]{:S(2)}) %copy-start.1) | copy-done | bytes 1835032
  4.5 0.0 copy-start.2
  4.5 1.5 %copy-done.2 = bf16[256,3584]{1,0:T(8,128)(2,1)S(1)} copy-done((bf16[256,3584]{1,0:T(8,128)(2,1)S(1)}, bf16[256,3584]{1,0:T(8,128)(2,1)}, u32[]{:S(2)}) %copy-start.2) | copy-done | bytes 1835032
  6.0 0.0 copy-start.3
  6.0 0.8 %copy-done.3 = bf16[8,3584]{1,0:T(8,128)(2,1)S(1)} copy-done((bf16[8,3584]{1,0:T(8,128)(2,1)S(1)}, bf16[8,3584]{1,0:T(8,128)(2,1)}, u32[]{:S(2)}) %copy-start.3) | copy-done | bytes 57368
  6.8 30.2 %shard_map.91 = bf16[8,3584]{1,0:T(8,128)(2,1)S(1)} custom-call(bf16[8,3584]{1,0:T(8,128)(2,1)S(1)} %copy-done.3, s32[8,4]{1,0:T(8,128)S(1)} %copy.10.ids_ref, f32[8,4]{1,0:T(8,128)S(1)} %copy.11.val_ref, bf16[3584,256]{1,0:T(8,128)(2,1)S(1)} %copy-done, bf16[3584,256]{1,0:T(8,128)(2,1)S(1)} %copy-done.1, bf16[256,3584]{1,0:T(8,128)(2,1)S(1)} %copy-done.2, ...), custom_call_target="tpu_custom_call" | custom-call | flops 704643072 | bytes 11010048 | tf_op jit(solution)/shard_map/pallas_call | solution.py:256
  37.1 0.6 %copy.13 = bf16[8,3584]{1,0:T(8,128)(2,1)} copy(bf16[8,3584]{1,0:T(8,128)(2,1)S(1)} %shard_map.91) | data formatting | bytes 114688
Async XLA Ops:
  1.5 1.5 %copy-start = (bf16[3584,256]{1,0:T(8,128)(2,1)S(1)}, bf16[3584,256]{1,0:T(8,128)(2,1)}, u32[]{:S(2)}) copy-start(bf16[3584,256]{1,0:T(8,128)(2,1)} %sg_ref.1) | copy-start | bytes 5505028
  3.0 1.5 %copy-start.1 = (bf16[3584,256]{1,0:T(8,128)(2,1)S(1)}, bf16[3584,256]{1,0:T(8,128)(2,1)}, u32[]{:S(2)}) copy-start(bf16[3584,256]{1,0:T(8,128)(2,1)} %su_ref.1) | copy-start | bytes 5505028
  4.5 1.5 %copy-start.2 = (bf16[256,3584]{1,0:T(8,128)(2,1)S(1)}, bf16[256,3584]{1,0:T(8,128)(2,1)}, u32[]{:S(2)}) copy-start(bf16[256,3584]{1,0:T(8,128)(2,1)} %sd_ref.1) | copy-start | bytes 5505028
  6.0 0.8 %copy-start.3 = (bf16[8,3584]{1,0:T(8,128)(2,1)S(1)}, bf16[8,3584]{1,0:T(8,128)(2,1)}, u32[]{:S(2)}) copy-start(bf16[8,3584]{1,0:T(8,128)(2,1)} %tok_ref.1) | copy-start | bytes 172036

commit v2 on v1

--- a/solution.py
+++ b/solution.py
@@ -123,11 +123,17 @@
 
     lane = lax.broadcasted_iota(jnp.int32, (tok, 128), 1)
     lane_expert = lax.rem(lane, experts)
+    across = lax.broadcasted_iota(jnp.int32, (tok, tok), 1)
+    diagonal = lax.broadcasted_iota(jnp.int32, (tok, tok), 0) == across
+
+    def column(line):
+        return jnp.sum(jnp.where(diagonal, line, 0.0), axis=1, keepdims=True)
+
+    lane_expert = lane_expert.astype(jnp.float32)
     weight = jnp.zeros((tok, 128), jnp.float32)
-    for k in range(ids_ref.shape[1]):
-        weight = weight + jnp.where(
-            ids_ref[:, k:k + 1] == lane_expert, val_ref[:, k:k + 1], jnp.float32(0.0)
-        )
+    for k in range(ids_ref.shape[0]):
+        name = column(ids_ref[k:k + 1, :].astype(jnp.float32))
+        weight = weight + jnp.where(name == lane_expert, column(val_ref[k:k + 1, :]), 0.0)
     high = weight.astype(jnp.bfloat16).astype(jnp.float32)
     middle = (weight - high).astype(jnp.bfloat16).astype(jnp.float32)
     low = weight - high - middle
@@ -278,14 +284,14 @@
             pltpu.SemaphoreType.DMA((copies,)),
         ],
         compiler_params=pltpu.CompilerParams(
-            collective_id=0, has_side_effects=True, vmem_limit_bytes=48 << 20
+            collective_id=0, has_side_effects=True, vmem_limit_bytes=60 << 20
         ),
         cost_estimate=pl.CostEstimate(
             flops=6 * tok * nodes * locals_ * width * hidden,
             bytes_accessed=2 * 3 * width * (hidden + shared_hidden),
             transcendentals=0,
         ),
-    )(*args)
+    )(tokens, expert_ids.T, args[2].T, *args[3:])
 
 
 def shards(*args):

time: 38 us -> 32.7 us (0.86)
  local copies, waits for them, and re-layouts: 7.45 us -> 1.45 us
  Pallas kernels: 30.2 us -> 31.1 us
    unnamed x11 -> x1, local copies, waits for them, and re-layouts: 7.45 us -> 1.45 us
    pallas_call x1, Pallas kernels: 30.2 us -> 31.1 us  [dense_shards(): pl.pallas_call(functools.partial(dense_kernel, (nodes, locals_, width, ex...]
where the time goes in v2:
time: 32.7 us; the launch traced here: 32.5 us
  Pallas kernels  31.1 us (95%)
  local copies, waits for them, and re-layouts  1.45 us (4%)
    pallas_call x1, Pallas kernels, dense_shards(): pl.pallas_call(functools.partial(dense_kernel, (nodes, locals_, width, ex...  31.1 us
    unnamed x1, local copies, waits for them, and re-layouts  1.45 us

profile of v2, /device:TPU:0, one launch (start us, length us, event | category | flops | bytes accessed | tf_op | source)
XLA Modules:
  0.0 32.5 jit_solution(15562947887309171175)
XLA Ops:
  0.0 31.1 %shard_map.91 = bf16[8,3584]{1,0:T(8,128)(2,1)} custom-call(bf16[8,3584]{1,0:T(8,128)(2,1)} %tok_ref.1, s32[4,8]{1,0:T(4,128)} %bitcast.2, f32[4,8]{1,0:T(4,128)} %bitcast.3, bf16[3584,256]{1,0:T(8,128)(2,1)} %sg_ref.1, bf16[3584,256]{1,0:T(8,128)(2,1)} %su_ref.1, bf16[256,3584]{1,0:T(8,128)(2,1)} %sd_ref.1, bf16[1,3584,256]{2,1,0:T(8,128)(2,1)} %eg_ref.1, ...), custom_call_target="tpu_custom_call" | custom-call | flops 704643072 | bytes 11010048 | tf_op jit(solution)/shard_map/pallas_call | solution.py:262
  31.1 1.4 %copy.11 = bf16[8,3584]{1,0:T(8,128)(2,1)} copy(bf16[8,3584]{1,0:T(8,128)(2,1)} %shard_map.91) | data formatting | bytes 114688

commit v3 on v2

--- a/solution.py
+++ b/solution.py
@@ -83,7 +83,7 @@
     tok_ref, ids_ref, val_ref, sg_ref, su_ref, sd_ref, eg_ref, eu_ref, ed_ref,
     out_ref,
     rows, sg, su, sd, eg, eu, ed,
-    keep, sib_out, sib_in, x_out, x_in, z_out, z_in,
+    shared, keep, sib_out, sib_in, x_out, x_in, z_out, z_in,
     load_sem, send_sem, recv_sem,
 ):
     nodes, locals_, width, experts = dims
@@ -91,7 +91,7 @@
     node, local = lax.axis_index("node"), lax.axis_index("local")
     evens = range(0, nodes, 2)
     far = range(2, nodes, 2)
-    order = list(range(locals_ - 1, 0, -1))
+    order = list(range(1, locals_))
 
     count = iter(range(1 << 16))
     id_z = {k: next(count) for k in order}
@@ -157,21 +157,6 @@
         started.append(copy)
         return copy
 
-    along_z, along_x, to_core = {}, {}, {}
-    for k in order:
-        along_z[k] = send(rows.at[0, 0], rows.at[0, k], id_z[k], at_local(k))
-
-    def pass_on(k):
-        for r in far:
-            along_x[r, k] = send(rows.at[0, k], rows.at[r, k], id_x[r, k], at_node(r))
-        to_core[0, k] = send(rows.at[0, k], rows.at[1, k], id_s[0, k], at_node(1))
-
-    arrival = list(range(locals_))
-    pass_on(0)
-    for k in arrival[1:]:
-        along_z[k].wait_recv()
-        pass_on(k)
-
     own_expert = (node * locals_ + local) // SHARDS
 
     def block(x, w_gate, w_up, w_down):
@@ -180,67 +165,93 @@
         h = (g / (1.0 + jnp.exp(-g)) * u).astype(jnp.bfloat16)
         return jnp.dot(h, w_down[...], preferred_element_type=jnp.float32)
 
-    def partial(r):
-        held = rows[r].astype(jnp.float32).reshape(locals_ * tok, width + 128)
+    along_z, along_x, to_core = {}, {}, {}
+    core_sums, x_sums, z_sums = {}, {}, {}
+
+    def gather_z(k):
+        along_z[k] = send(rows.at[0, 0], rows.at[k, 0], id_z[k], at_local(k))
+
+    def pass_own(k):
+        if k:
+            along_z[k].wait_recv()
+        for r in far:
+            along_x[r, k] = send(rows.at[k, 0], rows.at[k, r], id_x[r, k], at_node(r))
+        to_core[0, k] = send(rows.at[k, 0], rows.at[k, 1], id_s[0, k], at_node(1))
+
+    def pass_far(k):
+        for r in far:
+            along_x[r, k].wait_recv()
+            to_core[r, k] = send(rows.at[k, r], rows.at[k, r + 1], id_s[r, k], at_node(1))
+
+    def shared_terms():
+        held = jnp.concatenate([rows[k, 0].astype(jnp.float32) for k in range(locals_)], axis=0)
+        y = block(held[:, :width].astype(jnp.bfloat16), sg, su, sd)
+        shared[...] = y.reshape(locals_, tok, width)
+
+    def compute(k):
+        for r in evens:
+            to_core[r, k].wait_recv()
+        held = rows[k].astype(jnp.float32).reshape(nodes * tok, width + 128)
         x = held[:, :width].astype(jnp.bfloat16)
         tail = held[:, width:]
         lanes = lax.broadcasted_iota(jnp.int32, tail.shape, 1)
         mine = (lax.rem(lanes, experts) == own_expert) & (lanes < 3 * experts)
         factor = jnp.sum(jnp.where(mine, tail, 0.0), axis=1, keepdims=True)
-        y = block(x, eg, eu, ed) * factor
-        if r == 0:
-            y = y + block(x, sg, su, sd)
-        return y.reshape(locals_, tok, width)
-
-    core_sums = {}
-
-    def do_chunk(r):
-        y = partial(r)
-        if r % 2:
-            sib_out[r // 2] = y.astype(jnp.bfloat16)
-            for k in order + [0]:
-                core_sums[r - 1, k] = send(
-                    sib_out.at[r // 2, k], sib_in.at[r // 2, k], id_rs[r - 1, k], at_node(1)
-                )
-        else:
-            keep[r // 2] = y
-
-    for load in loads[1:]:
-        load.wait()
-    do_chunk(0)
-    for r in far:
-        for k in arrival:
-            along_x[r, k].wait_recv()
-            to_core[r, k] = send(rows.at[r, k], rows.at[r + 1, k], id_s[r, k], at_node(1))
-    for k in arrival:
-        to_core[0, k].wait_recv()
-    do_chunk(1)
-    for r in far:
-        do_chunk(r)
-        for k in arrival:
-            to_core[r, k].wait_recv()
-        do_chunk(r + 1)
-
-    x_sums, z_sums = {}, {}
-    for r in far:
-        for k in order + [0]:
+        y = (block(x, eg, eu, ed) * factor).reshape(nodes, tok, width)
+        for r in reversed(evens):
+            sib_out[k, r // 2] = y[r + 1].astype(jnp.bfloat16)
+            core_sums[r, k] = send(
+                sib_out.at[k, r // 2], sib_in.at[k, r // 2], id_rs[r, k], at_node(1)
+            )
+            keep[k, r // 2] = y[r]
+
+    def sum_x(k):
+        for r in far:
             core_sums[r, k].wait_recv()
-            x_out[r // 2 - 1, k] = (
-                keep[r // 2, k] + sib_in[r // 2, k].astype(jnp.float32)
+            x_out[k, r // 2 - 1] = (
+                keep[k, r // 2] + sib_in[k, r // 2].astype(jnp.float32)
             ).astype(jnp.bfloat16)
             x_sums[r, k] = send(
-                x_out.at[r // 2 - 1, k], x_in.at[r // 2 - 1, k], id_rx[r, k], at_node(r)
+                x_out.at[k, r // 2 - 1], x_in.at[k, r // 2 - 1], id_rx[r, k], at_node(r)
             )
-    for k in order + [0]:
+
+    def sum_z(k):
         core_sums[0, k].wait_recv()
-        total = keep[0, k] + sib_in[0, k].astype(jnp.float32)
+        total = shared[k] + keep[k, 0] + sib_in[k, 0].astype(jnp.float32)
         for r in far:
             x_sums[r, k].wait_recv()
-            total = total + x_in[r // 2 - 1, k].astype(jnp.float32)
+            total = total + x_in[k, r // 2 - 1].astype(jnp.float32)
         if k:
             z_out[k] = total.astype(jnp.bfloat16)
             z_sums[k] = send(z_out.at[k], z_in.at[k], id_rz[k], at_local(k))
-    for k in reversed(order):
+        else:
+            shared[k] = total
+
+    for k in order:
+        gather_z(k)
+    arrival = [0] + order
+    count = len(arrival)
+    pass_own(0)
+    for i in range(1, count):
+        pass_own(arrival[i])
+        if i <= 1:
+            pass_far(arrival[0])
+    for load in loads[1:]:
+        load.wait()
+    for i in range(1, count + 2):
+        if i < count:
+            pass_far(arrival[i])
+        if i <= count:
+            compute(arrival[i - 1])
+        if 2 <= i:
+            if i == count + 1:
+                shared_terms()
+            sum_x(arrival[i - 2])
+    for k in order:
+        sum_z(k)
+    sum_z(0)
+    total = shared[0]
+    for k in order:
         z_sums[k].wait_recv()
         total = total + z_in[k].astype(jnp.float32)
     out_ref[...] = total.astype(jnp.bfloat16)
@@ -265,18 +276,19 @@
         in_specs=[any_spec, vmem_spec, vmem_spec] + [any_spec] * 6,
         out_specs=vmem_spec,
         scratch_shapes=[
-            pltpu.VMEM((nodes, locals_, tok, width + 128), bf16),
+            pltpu.VMEM((locals_, nodes, tok, width + 128), bf16),
             pltpu.VMEM((width, shared_hidden), bf16),
             pltpu.VMEM((width, shared_hidden), bf16),
             pltpu.VMEM((shared_hidden, width), bf16),
             pltpu.VMEM((width, hidden), bf16),
             pltpu.VMEM((width, hidden), bf16),
             pltpu.VMEM((hidden, width), bf16),
-            pltpu.VMEM((pairs, locals_, tok, width), f32),
-            pltpu.VMEM((pairs, locals_, tok, width), bf16),
-            pltpu.VMEM((pairs, locals_, tok, width), bf16),
-            pltpu.VMEM((pairs - 1, locals_, tok, width), bf16),
-            pltpu.VMEM((pairs - 1, locals_, tok, width), bf16),
+            pltpu.VMEM((locals_, tok, width), f32),
+            pltpu.VMEM((locals_, pairs, tok, width), f32),
+            pltpu.VMEM((locals_, pairs, tok, width), bf16),
+            pltpu.VMEM((locals_, pairs, tok, width), bf16),
+            pltpu.VMEM((locals_, pairs - 1, tok, width), bf16),
+            pltpu.VMEM((locals_, pairs - 1, tok, width), bf16),
             pltpu.VMEM((locals_, tok, width), bf16),
             pltpu.VMEM((locals_, tok, width), bf16),
             pltpu.SemaphoreType.DMA((7,)),

time: 32.7 us -> 30 us (0.917)
  Pallas kernels: 31.1 us -> 28.4 us
    pallas_call x1, Pallas kernels: 31.1 us -> 28.4 us  [dense_shards(): pl.pallas_call(functools.partial(dense_kernel, (nodes, locals_, width, ex...]
where the time goes in v3:
time: 30 us; the launch traced here: 29.8 us
  Pallas kernels  28.4 us (95%)
  local copies, waits for them, and re-layouts  1.45 us (5%)
    pallas_call x1, Pallas kernels, dense_shards(): pl.pallas_call(functools.partial(dense_kernel, (nodes, locals_, width, ex...  28.4 us
    unnamed x1, local copies, waits for them, and re-layouts  1.45 us

profile of v3, /device:TPU:0, one launch (start us, length us, event | category | flops | bytes accessed | tf_op | source)
XLA Modules:
  0.0 29.8 jit_solution(11113869575719688351)
XLA Ops:
  0.0 28.4 %shard_map.91 = bf16[8,3584]{1,0:T(8,128)(2,1)} custom-call(bf16[8,3584]{1,0:T(8,128)(2,1)} %tok_ref.1, s32[4,8]{1,0:T(4,128)} %bitcast.2, f32[4,8]{1,0:T(4,128)} %bitcast.3, bf16[3584,256]{1,0:T(8,128)(2,1)} %sg_ref.1, bf16[3584,256]{1,0:T(8,128)(2,1)} %su_ref.1, bf16[256,3584]{1,0:T(8,128)(2,1)} %sd_ref.1, bf16[1,3584,256]{2,1,0:T(8,128)(2,1)} %eg_ref.1, ...), custom_call_target="tpu_custom_call" | custom-call | flops 704643072 | bytes 11010048 | tf_op jit(solution)/shard_map/pallas_call | solution.py:273
  28.4 1.4 %copy.11 = bf16[8,3584]{1,0:T(8,128)(2,1)} copy(bf16[8,3584]{1,0:T(8,128)(2,1)} %shard_map.91) | data formatting | bytes 114688

commit v4 on v3

--- a/solution.py
+++ b/solution.py
@@ -244,9 +244,8 @@
         if i <= count:
             compute(arrival[i - 1])
         if 2 <= i:
-            if i == count + 1:
-                shared_terms()
             sum_x(arrival[i - 2])
+    shared_terms()
     for k in order:
         sum_z(k)
     sum_z(0)

time: 30 us -> 30.7 us (1.023)
  Pallas kernels: 28.4 us -> 29 us
    pallas_call x1, Pallas kernels: 28.4 us -> 29 us  [dense_shards(): pl.pallas_call(functools.partial(dense_kernel, (nodes, locals_, width, ex...]
where the time goes in v4:
time: 30.7 us; the launch traced here: 30.5 us
  Pallas kernels  29 us (94%)
  local copies, waits for them, and re-layouts  1.45 us (5%)
    pallas_call x1, Pallas kernels, dense_shards(): pl.pallas_call(functools.partial(dense_kernel, (nodes, locals_, width, ex...  29 us
    unnamed x1, local copies, waits for them, and re-layouts  1.45 us

profile of v4, /device:TPU:0, one launch (start us, length us, event | category | flops | bytes accessed | tf_op | source)
XLA Modules:
  0.0 30.5 jit_solution(1733887193970035352)
XLA Ops:
  0.0 29.0 %shard_map.91 = bf16[8,3584]{1,0:T(8,128)(2,1)} custom-call(bf16[8,3584]{1,0:T(8,128)(2,1)} %tok_ref.1, s32[4,8]{1,0:T(4,128)} %bitcast.2, f32[4,8]{1,0:T(4,128)} %bitcast.3, bf16[3584,256]{1,0:T(8,128)(2,1)} %sg_ref.1, bf16[3584,256]{1,0:T(8,128)(2,1)} %su_ref.1, bf16[256,3584]{1,0:T(8,128)(2,1)} %sd_ref.1, bf16[1,3584,256]{2,1,0:T(8,128)(2,1)} %eg_ref.1, ...), custom_call_target="tpu_custom_call" | custom-call | flops 704643072 | bytes 11010048 | tf_op jit(solution)/shard_map/pallas_call | solution.py:272
  29.0 1.4 %copy.11 = bf16[8,3584]{1,0:T(8,128)(2,1)} copy(bf16[8,3584]{1,0:T(8,128)(2,1)} %shard_map.91) | data formatting | bytes 114688
